TPU v7x, 256 devices: a whole 4x4x8 slice. The times are simulated.
256 devices in a mesh: vox: 32 (over z, y), col: 8 (over x, core).
Axes of the slice: x: 4, y: 4, z: 8, core: 2. Of those that a mesh axis runs over, the one named last changes fastest.
Arguments:
- start_modes: float32 [128, 131072], P('col', 'vox'), may hold values from -48 to 48
- start_dirs: float32 [128, 131072], P('col', 'vox'), may hold values from -6 to 6
- coupling: float32 [13, 131072], P(None, ('vox', 'col')), may hold values from 0.05 to 1
- relax_class: int32 [131072], P(('vox', 'col')), may hold values from 0 to 3
- relaxivity: float32 [4], replicated, may hold values from 0.5 to 4
Outputs:
- modes: float32 [128, 131072], P('col', 'vox')
- ritz: float32 [128, 128], replicated
All inputs are finite; a program needn't handle non-finite values.
Results may differ from a plain program's by a relative error of at most 0.0003.
Values sent between devices are 32-bit elements; how exact they have to be, the bound alone decides.
A program may use at most 64 MiB of HBM per device.

v0:
```python
import math
import jax
import jax.numpy as jnp
from jax import lax
from jax.sharding import PartitionSpec as P

NX = 256
NZ = 2
HALF = 13
ITERS = 2
QSTEPS = 3
offsets = [
    (a, b, c) for a in (-1, 0, 1) for b in (-1, 0, 1) for c in (-1, 0, 1) if (a, b, c) > (0, 0, 0)
]


def from_behind(block, axis, distance):
    devices = range(lax.axis_size(axis))
    route = [(i - distance, i) for i in devices if i - distance in devices]
    return lax.ppermute(block, axis, route)


def extended_2(block, sides, width):
    for axis, dim in sides:
        count = lax.axis_size(axis)
        forward = [(i, i + 1) for i in range(count - 1)]
        backward = [(target, source) for source, target in forward]
        low = lax.ppermute(
            lax.slice_in_dim(block, block.shape[dim] - width, None, axis=dim), axis, forward
        )
        high = lax.ppermute(lax.slice_in_dim(block, 0, width, axis=dim), axis, backward)
        block = jnp.concatenate([low, block, high], axis=dim)
    return block


def matmul(left, right):
    return jnp.dot(left, right, precision=lax.Precision.HIGHEST, preferred_element_type=jnp.float32)


def lower_solve(lower, rhs):
    return lax.linalg.triangular_solve(lower, rhs, left_side=True, lower=True)


def upper_solve(lower, rhs):
    return lax.linalg.triangular_solve(lower, rhs, left_side=True, lower=True, transpose_a=True)


def symmetric(matrix):
    return 0.5 * (matrix + matrix.T)


def project_pencil(gram_a, gram_b, count):
    sym_a = symmetric(gram_a)
    scales = lax.rsqrt(jnp.diagonal(gram_b) + 1e-06)
    normed_b = scales[:, None] * gram_b * scales[None, :]
    normed_a = scales[:, None] * sym_a * scales[None, :]
    lower = jnp.linalg.cholesky(normed_b)
    half_way = lower_solve(lower, normed_a)
    reduced = lower_solve(lower, half_way.T)
    shift = 2.0 * jnp.max(jnp.sum(jnp.abs(reduced), axis=1))
    iterate = jnp.eye(gram_a.shape[0], count, dtype=jnp.float32)
    for sweep_index in range(QSTEPS):
        iterate = shift * iterate - matmul(reduced, iterate)
        factor = jnp.linalg.cholesky(matmul(iterate.T, iterate))
        iterate = lower_solve(factor, iterate.T).T
    return scales[:, None] * upper_solve(lower, iterate)


def neighbour_sum(padded, coupled):
    rows_y = padded.shape[1] - 2
    rows_z = padded.shape[2] - 2
    rows_x = padded.shape[3] - 2
    total = jnp.zeros((padded.shape[0], rows_y, rows_z, rows_x), jnp.float32)
    for which, (step_y, step_z, step_x) in enumerate(offsets):
        ahead = padded[
            :,
            1 + step_y : 1 + step_y + rows_y,
            1 + step_z : 1 + step_z + rows_z,
            1 + step_x : 1 + step_x + rows_x,
        ]
        behind = padded[
            :,
            1 - step_y : 1 - step_y + rows_y,
            1 - step_z : 1 - step_z + rows_z,
            1 - step_x : 1 - step_x + rows_x,
        ]
        here = coupled[which, 1 : 1 + rows_y, 1 : 1 + rows_z, 1 : 1 + rows_x]
        back = coupled[
            which,
            1 - step_y : 1 - step_y + rows_y,
            1 - step_z : 1 - step_z + rows_z,
            1 - step_x : 1 - step_x + rows_x,
        ]
        total = total + here[None] * ahead
        total = total + back[None] * behind
    return total


def pad_plane(array):
    return jnp.pad(array, ((0, 0), (0, 0), (1, 1), (1, 1)))


def quotient(modes, images):
    total = lax.psum(matmul(modes, images.T), ("vox", "col"))
    return symmetric(total)


def on_device(start_modes, start_dirs, coupling, relax_class, relaxivity):
    local_voxels = coupling.shape[1]
    match = relax_class[:, None] == jnp.arange(relaxivity.shape[0], dtype=jnp.int32)[None, :]
    voxel_rate = jnp.sum(jnp.where(match, relaxivity[None, :], jnp.float32(0.0)), axis=1)
    damping = 1.0 / (1.0 + voxel_rate)
    own_coupling = coupling.reshape(HALF, 1, NZ, NX)
    before = from_behind(own_coupling, ("vox", "col"), 1)
    coupled = pad_plane(
        jnp.concatenate([before, own_coupling, jnp.zeros_like(own_coupling)], axis=1)
    )
    position = lax.axis_index(("vox", "col"))
    device_count = lax.axis_size(("vox", "col"))
    plane = jnp.ones((1, 1, NZ, NX), jnp.float32)
    upper_flag = (position > 0).astype(jnp.float32)
    lower_flag = (position < device_count - 1).astype(jnp.float32)
    unity = pad_plane(jnp.concatenate([upper_flag * plane, plane, lower_flag * plane], axis=1))
    degree = neighbour_sum(unity, coupled).reshape(local_voxels)
    diagonal = degree + voxel_rate

    def operate(field):
        count = field.shape[0]
        shaped = field.reshape(count, 1, NZ, NX)
        extended = extended_2(shaped, ((("vox", "col"), 1),), 1)
        padded = pad_plane(extended)
        return diagonal[None, :] * field - neighbour_sum(padded, coupled).reshape(
            count, local_voxels
        )

    modes, dirs = (
        lax.all_to_all(start_modes, "col", split_axis=1, concat_axis=0, tiled=True),
        lax.all_to_all(start_dirs, "col", split_axis=1, concat_axis=0, tiled=True),
    )
    count = modes.shape[0]
    images = operate(modes)
    dir_images = operate(dirs)
    ritz = quotient(modes, images)
    for iteration in range(ITERS):
        resid = images - matmul(ritz, modes)
        search = resid * damping[None, :]
        search_images = operate(search)
        basis = jnp.concatenate([modes, search, dirs], axis=0)
        basis_images = jnp.concatenate([images, search_images, dir_images], axis=0)
        local_a = matmul(basis, basis_images.T)
        local_b = matmul(basis, basis.T)
        gram_a, gram_b = lax.psum((local_a, local_b), ("vox", "col"))
        coeffs = project_pencil(gram_a, gram_b, count)
        modes = matmul(coeffs.T, basis)
        images = matmul(coeffs.T, basis_images)
        dirs = matmul(coeffs[count:].T, basis[count:])
        dir_images = matmul(coeffs[count:].T, basis_images[count:])
        ritz = quotient(modes, images)
    total_voxels = device_count * local_voxels
    scaled = modes * math.sqrt(total_voxels)
    modes_out = lax.all_to_all(scaled, "col", split_axis=0, concat_axis=1, tiled=True)
    return (modes_out, ritz)


def solution(mesh):
    in_specs = (P("col", "vox"), P("col", "vox"), P(None, ("vox", "col")), P(("vox", "col")), P())
    out_specs = (P("col", "vox"), P())
    return jax.shard_map(
        on_device, mesh=mesh, in_specs=in_specs, out_specs=out_specs, check_vma=False
    )
```

profile of v0, /device:TPU:1, one launch (start us, length us, event | category | flops | bytes accessed | tf_op | source)
XLA Modules:
  0.0 1733.3 jit_solution(11976527018198322847)
XLA Ops:
  7.2 1.7 copy.120
  8.8 6.6 all-to-all-start
  16.2 3.5 collective-permute-start
  22.8 1.7 copy.119
  25.2 4.1 all-to-all-start.1
  29.5 2.0 collective-permute-start.2
  31.4 3.6 collective-permute-start.1
  36.0 2.9 collective-permute-start.6
  38.9 2.6 collective-permute-start.5
  41.6 2.3 select_maximum_fusion.6
  43.9 4.5 multiply_subtract_fusion.3
  49.6 3.4 select_maximum_fusion.2
  53.1 245.1 %all-reduce.15.cloned.1.call-done = f32[128,128]{0,1:T(8,128)} async-done(((f32[128,128]{0,1:T(8,128)}), f32[128,128]{0,1:T(8,128)}) %all-reduce.15.cloned.1.call-update) | async-done | bytes 65552 | tf_op jit(solution)/shard_map/psum | solution.py:104
  301.3 2.0 collective-permute-start.4
  303.3 3.9 collective-permute-start.3
  307.2 5.4 fusion.64
  312.7 2.2 fusion.38
  314.9 2.3 select_maximum_fusion.4
  317.3 4.4 fusion.89
  322.7 2.3 fusion.14
  325.0 256.1 %all-reduce.23.cloned.1.call-done = (f32[384,384]{1,0:T(8,128)}, f32[384,384]{0,1:T(8,128)}) async-done(((f32[384,384]{1,0:T(8,128)}, f32[384,384]{0,1:T(8,128)}), (f32[384,384]{1,0:T(8,128)}, f32[384,384]{0,1:T(8,128)})) %all-reduce.23.cloned.1.call-update) | async-done | bytes 1179664 | tf_op jit(solution)/shard_map/psum | solution.py:152
  581.2 6.6 gather_fusion
  590.4 11.7 cholesky.310
  602.2 9.8 custom-call.40
  614.4 11.7 cholesky.329
  626.2 9.9 custom-call.41
  637.5 11.7 cholesky.348
  652.6 5.9 while.12
  653.2 1.3 bitcast_dynamic-update-slice_fusion.4
  658.5 29.7 %custom-call.47 = f32[3,128,128]{1,2,0:T(8,128)S(1)} custom-call(f32[3,128,128]{2,1,0:T(8,128)S(1)} %get-tuple-element.49), custom_call_target="InvertDiagBlocksLowerTriangular" | custom-call | tf_op jit(solution)/shard_map/triangular_solve/custom-call.8 | solution.py:45
  695.7 11.7 cholesky.361
  708.7 9.8 custom-call.44
  720.8 11.7 cholesky.372
  733.9 9.8 custom-call.45
  745.5 11.9 cholesky.383
  758.7 9.8 custom-call.46
  773.6 237.5 %all-reduce.17.cloned.1.call-done = f32[128,128]{1,0:T(8,128)} async-done(((f32[128,128]{1,0:T(8,128)}), f32[128,128]{1,0:T(8,128)}) %all-reduce.17.cloned.1.call-update) | async-done | bytes 65552 | tf_op jit(solution)/shard_map/psum | solution.py:104
  1013.5 1.9 collective-permute-start.8
  1015.4 3.6 collective-permute-start.7
  1019.5 2.2 fusion.36
  1022.4 2.3 select_maximum_fusion
  1024.6 4.4 fusion.39
  1029.2 2.3 fusion.12
  1031.5 259.7 %all-reduce.21.cloned.1.call-done = (f32[384,384]{1,0:T(8,128)}, f32[384,384]{0,1:T(8,128)}) async-done(((f32[384,384]{1,0:T(8,128)}, f32[384,384]{0,1:T(8,128)}), (f32[384,384]{1,0:T(8,128)}, f32[384,384]{0,1:T(8,128)})) %all-reduce.21.cloned.1.call-update) | async-done | bytes 1179664 | tf_op jit(solution)/shard_map/psum | solution.py:152
  1291.2 6.6 gather_fusion.1
  1300.6 11.7 cholesky.396
  1312.4 9.8 custom-call.48
  1324.5 11.7 cholesky.415
  1336.3 10.2 custom-call.49
  1347.8 11.7 cholesky.434
  1363.5 6.4 while.13
  1364.2 1.4 bitcast_dynamic-update-slice_fusion.5
  1366.3 1.4 bitcast_dynamic-update-slice_fusion.5
  1368.4 1.4 bitcast_dynamic-update-slice_fusion.5
  1369.9 29.7 %custom-call.55 = f32[3,128,128]{1,2,0:T(8,128)S(1)} custom-call(f32[3,128,128]{2,1,0:T(8,128)S(1)} %get-tuple-element.52), custom_call_target="InvertDiagBlocksLowerTriangular" | custom-call | tf_op jit(solution)/shard_map/triangular_solve/custom-call.8 | solution.py:45
  1407.1 11.7 cholesky.447
  1420.1 9.8 custom-call.52
  1432.0 11.7 cholesky.458
  1445.0 9.8 custom-call.53
  1456.7 11.9 cholesky.469
  1470.0 9.8 custom-call.54
  1481.7 1.4 broadcast_multiply_fusion
  1485.0 7.1 all-to-all-start.2
  1492.1 231.0 %all-reduce.19.cloned.1.call-done = f32[128,128]{1,0:T(8,128)} async-done(((f32[128,128]{1,0:T(8,128)}), f32[128,128]{1,0:T(8,128)}) %all-reduce.19.cloned.1.call-update) | async-done | bytes 65552 | tf_op jit(solution)/shard_map/psum | solution.py:104
  (313 shorter events, 78.5 us)
Async XLA Ops:
  8.8 16.4 all-to-all-start
  16.2 8.8 collective-permute-start
  25.2 10.6 all-to-all-start.1
  29.3 268.9 %all-reduce.15.cloned.1.call-start = ((), (), s32[]{:S(2)}) async-start(), calls=%async_computation.3 | async-start | bytes 131072 | tf_op jit(solution)/shard_map/psum | solution.py:104
  29.5 12.1 collective-permute-start.2
  31.4 10.1 collective-permute-start.1
  35.1 13.3 copy-start.21
  35.1 13.3 copy-start.23
  35.1 13.3 copy-start.25
  35.1 13.3 copy-start.27
  35.2 13.3 copy-start.29
  35.2 13.3 copy-start.31
  35.2 13.3 copy-start.33
  35.8 17.2 copy-start.35
  36.0 12.5 copy-start.15
  36.0 13.6 collective-permute-start.6
  38.9 10.7 collective-permute-start.5
  49.6 531.6 %all-reduce.23.cloned.1.call-start = ((), (), s32[]{:S(2)}) async-start(), calls=%async_computation.7 | async-start | bytes 2359296 | tf_op jit(solution)/shard_map/psum | solution.py:152
  49.6 3.4 copy-start.14
  301.3 13.6 copy-start.16
  301.3 13.6 collective-permute-start.4
  303.3 11.6 collective-permute-start.3
  312.6 4.6 copy-start.22
  312.6 4.6 copy-start.24
  312.6 4.6 copy-start.26
  312.6 4.6 copy-start.28
  312.6 4.6 copy-start.30
  312.6 4.6 copy-start.32
  312.7 4.6 copy-start.34
  317.3 4.5 copy-start.36
  321.9 0.7 copy-start.6
  321.9 0.8 copy-start.8
  325.0 686.1 %all-reduce.17.cloned.1.call-start = ((), (), s32[]{:S(2)}) async-start(), calls=%async_computation.4 | async-start | bytes 131072 | tf_op jit(solution)/shard_map/psum | solution.py:104
  581.2 6.6 copy-start.2
  581.2 7.7 copy-start
  590.4 11.7 copy-start.12
  744.1 26.5 %copy-start.7 = (f32[128,512]{1,0:T(8,128)S(1)}, f32[128,512]{1,0:T(8,128)}, u32[]{:S(2)}) copy-start(f32[128,512]{1,0:T(8,128)} %copy-done.6) | copy-start | bytes 786436
  744.1 26.5 %copy-start.9 = (f32[128,512]{1,0:T(8,128)S(1)}, f32[128,512]{1,0:T(8,128)}, u32[]{:S(2)}) copy-start(f32[128,512]{1,0:T(8,128)} %copy-done.8) | copy-start | bytes 786436
  770.2 241.8 %copy-start.37 = (f32[512]{0:T(512)S(1)}, f32[512]{0:T(512)}, u32[]{:S(2)}) copy-start(f32[512]{0:T(512)} %get-tuple-element.163) | copy-start | bytes 6148
  771.3 257.8 %copy-start.4 = (f32[128,512]{1,0:T(8,128)}, f32[128,512]{1,0:T(8,128)S(1)}, u32[]{:S(2)}) copy-start(f32[128,512]{1,0:T(8,128)S(1)} %fusion.13) | copy-start | bytes 786436
  773.1 518.2 %all-reduce.21.cloned.1.call-start = ((), (), s32[]{:S(2)}) async-start(), calls=%async_computation.6 | async-start | bytes 2359296 | tf_op jit(solution)/shard_map/psum | solution.py:152
  773.6 255.6 %copy-start.10 = (f32[128,512]{1,0:T(8,128)}, f32[128,512]{1,0:T(8,128)S(1)}, u32[]{:S(2)}) copy-start(f32[128,512]{1,0:T(8,128)S(1)} %fusion.15) | copy-start | bytes 786436
  1013.5 8.3 collective-permute-start.8
  1015.4 6.9 collective-permute-start.7
  1019.5 9.7 copy-start.17
  1029.2 268.7 %copy-start.19 = (f32[128,512]{1,0:T(8,128)}, f32[128,512]{1,0:T(8,128)S(1)}, u32[]{:S(2)}) copy-start(f32[128,512]{1,0:T(8,128)S(1)} %multiply_subtract_fusion) | copy-start | bytes 786436
  1031.5 691.6 %all-reduce.19.cloned.1.call-start = ((), (), s32[]{:S(2)}) async-start(), calls=%async_computation.5 | async-start | bytes 131072 | tf_op jit(solution)/shard_map/psum | solution.py:104
  1291.2 6.7 copy-start.3
  1291.2 7.7 copy-start.1
  1300.5 11.7 copy-start.13
  1454.8 26.9 %copy-start.11 = (f32[128,512]{1,0:T(8,128)S(1)}, f32[128,512]{1,0:T(8,128)}, u32[]{:S(2)}) copy-start(f32[128,512]{1,0:T(8,128)} %copy-done.10) | copy-start | bytes 786436
  1455.9 27.2 %copy-start.5 = (f32[128,512]{1,0:T(8,128)S(1)}, f32[128,512]{1,0:T(8,128)}, u32[]{:S(2)}) copy-start(f32[128,512]{1,0:T(8,128)} %copy-done.4) | copy-start | bytes 786436
  1455.9 27.2 %copy-start.18 = (f32[128,512]{1,0:T(8,128)S(1)}, f32[128,512]{1,0:T(8,128)}, u32[]{:S(2)}) copy-start(f32[128,512]{1,0:T(8,128)} %copy-done.17) | copy-start | bytes 786436
  1455.9 27.2 %copy-start.20 = (f32[128,512]{1,0:T(8,128)S(1)}, f32[128,512]{1,0:T(8,128)}, u32[]{:S(2)}) copy-start(f32[128,512]{1,0:T(8,128)} %copy-done.19) | copy-start | bytes 786436
  1485.0 240.7 %all-to-all-start.2 = ((f32[8,16,512]{2,1,0:T(8,128)}), f32[8,16,512]{2,1,0:T(8,128)S(1)}, u32[]{:S(2)}, u32[]{:S(2)}) async-start(f32[8,16,512]{2,1,0:T(8,128)} %bitcast.87), calls=%async_computation.2 | async-start | bytes 524288 | tf_op jit(solution)/shard_map/all_to_all | solution.py:161
Sparse Core Ops, SparseCore 0:
  49.7 248.4 all-reduce.14
  325.1 256.0 all-reduce.22
  773.2 237.8 all-reduce.16
  1031.6 259.5 all-reduce.20
  1485.1 237.9 all-reduce.18
where the time goes:
time: 1740 us; the launch traced here: 1730 us
  waiting for transfers between devices  1230 us (71%)
  other arithmetic  348 us (20%)
  matrix products  48.7 us (3%)
  starting transfers between devices  44.1 us (3%)
  local copies, waits for them, and re-layouts  41.4 us (2%)
  between operations  21 us (1%)
    psum x3, waiting for transfers between devices, quotient(): total = lax.psum(matmul(modes, images.T), ('vox', 'col'))  714 us
    psum x2, waiting for transfers between devices, on_device(): gram_a, gram_b = lax.psum((local_a, local_b), ('vox', 'col'))  516 us
    another operation x21, other arithmetic, project_pencil(): lower = jnp.linalg.cholesky(normed_b)  114 us
    another operation x18, other arithmetic, project_pencil(): factor = jnp.linalg.cholesky(matmul(iterate.T, iterate))  74.7 us
    another operation x12, other arithmetic, lower_solve(): return lax.linalg.triangular_solve(lower, rhs, left_side=True, lower=True)  62.8 us
    another operation x5, other arithmetic, upper_solve(): lax.linalg.triangular_solve(lower, rhs, left_side=True, lower=True, trans...  59.5 us
  transfers between devices with their start and end apart: 17, of which 6 were waited for; matrix products, arithmetic and copies ran while one was open for 2% of the time, Pallas kernels for 0%

commit v1 on v0

--- a/solution.py
+++ b/solution.py
@@ -12,6 +12,11 @@
 offsets = [
     (a, b, c) for a in (-1, 0, 1) for b in (-1, 0, 1) for c in (-1, 0, 1) if (a, b, c) > (0, 0, 0)
 ]
+
+
+def one_after_other(x, axis_one, axis_two):
+    inner = lax.psum(x, axis_one)
+    return lax.psum(inner, axis_two)
 
 
 def from_behind(block, axis, distance):
@@ -101,7 +106,7 @@
 
 
 def quotient(modes, images):
-    total = lax.psum(matmul(modes, images.T), ("vox", "col"))
+    total = one_after_other(matmul(modes, images.T), "vox", "col")
     return symmetric(total)
 
 

time: 1740 us -> 1640 us (0.943)
  waiting for transfers between devices: 1230 us -> 1120 us
    psum x3 -> x6, waiting for transfers between devices: 714 us -> 600 us  [the longest x3 411 us: one_after_other(): inner = lax.psum(x, axis_one)]
  transfers between devices with their start and end apart: 17 -> 20, of which waited for: 6 -> 9; matrix products, arithmetic and copies ran while one was open for 2% -> 2% of each run, Pallas kernels for 0% -> 0%
where the time goes in v1:
time: 1640 us; the launch traced here: 1630 us
  waiting for transfers between devices  1120 us (68%)
  other arithmetic  349 us (21%)
  matrix products  48.7 us (3%)
  starting transfers between devices  48 us (3%)
  local copies, waits for them, and re-layouts  42.1 us (3%)
  between operations  21.3 us (1%)
    psum x2, waiting for transfers between devices, on_device(): gram_a, gram_b = lax.psum((local_a, local_b), ('vox', 'col'))  524 us
    psum x3, waiting for transfers between devices, one_after_other(): inner = lax.psum(x, axis_one)  411 us
    psum x3, waiting for transfers between devices, one_after_other(): return lax.psum(inner, axis_two)  188 us
    another operation x21, other arithmetic, project_pencil(): lower = jnp.linalg.cholesky(normed_b)  114 us
    another operation x18, other arithmetic, project_pencil(): factor = jnp.linalg.cholesky(matmul(iterate.T, iterate))  74.7 us
    another operation x12, other arithmetic, lower_solve(): return lax.linalg.triangular_solve(lower, rhs, left_side=True, lower=True)  62.8 us
    another operation x5, other arithmetic, upper_solve(): lax.linalg.triangular_solve(lower, rhs, left_side=True, lower=True, trans...  59.5 us
  transfers between devices with their start and end apart: 20, of which 9 were waited for; matrix products, arithmetic and copies ran while one was open for 2% of the time, Pallas kernels for 0%

profile of v1, /device:TPU:1, one launch (start us, length us, event | category | flops | bytes accessed | tf_op | source)
XLA Modules:
  0.0 1634.1 jit_solution(14013786607438789904)
XLA Ops:
  7.2 1.7 copy.120
  8.8 6.6 all-to-all-start
  16.2 3.5 collective-permute-start
  22.8 1.7 copy.119
  25.2 4.1 all-to-all-start.1
  29.5 2.0 collective-permute-start.2
  31.4 3.6 collective-permute-start.1
  36.0 2.9 collective-permute-start.6
  38.9 2.6 collective-permute-start.5
  41.6 2.3 select_maximum_fusion.6
  43.9 5.1 multiply_subtract_fusion.3
  50.2 3.4 select_maximum_fusion.2
  54.3 141.3 %all-reduce.18.cloned.1.call-done = f32[128,128]{0,1:T(8,128)} async-done(((f32[128,128]{0,1:T(8,128)}), f32[128,128]{0,1:T(8,128)}) %all-reduce.18.cloned.1.call-update) | async-done | bytes 65552 | tf_op jit(solution)/shard_map/psum | solution.py:18
  196.8 65.3 %all-reduce.20.cloned.1.call-done = f32[128,128]{0,1:T(8,128)} async-done(((f32[128,128]{0,1:T(8,128)}), f32[128,128]{0,1:T(8,128)}) %all-reduce.20.cloned.1.call-update) | async-done | bytes 65552 | tf_op jit(solution)/shard_map/psum | solution.py:19
  265.1 4.8 collective-permute-start.4
  269.9 2.1 collective-permute-start.3
  272.0 5.4 fusion.64
  277.5 2.2 fusion.38
  279.7 2.3 select_maximum_fusion.4
  282.1 4.4 fusion.89
  287.5 2.3 fusion.14
  289.9 260.7 %all-reduce.32.cloned.1.call-done = (f32[384,384]{1,0:T(8,128)}, f32[384,384]{0,1:T(8,128)}) async-done(((f32[384,384]{1,0:T(8,128)}, f32[384,384]{0,1:T(8,128)}), (f32[384,384]{1,0:T(8,128)}, f32[384,384]{0,1:T(8,128)})) %all-reduce.32.cloned.1.call-update) | async-done | bytes 1179664 | tf_op jit(solution)/shard_map/psum | solution.py:157
  550.6 6.6 gather_fusion
  559.8 11.7 cholesky.310
  571.6 9.8 custom-call.40
  583.8 11.7 cholesky.329
  595.6 9.9 custom-call.41
  606.8 11.7 cholesky.348
  622.0 5.9 while.12
  627.9 29.7 %custom-call.47 = f32[3,128,128]{1,2,0:T(8,128)S(1)} custom-call(f32[3,128,128]{2,1,0:T(8,128)S(1)} %get-tuple-element.49), custom_call_target="InvertDiagBlocksLowerTriangular" | custom-call | tf_op jit(solution)/shard_map/triangular_solve/custom-call.8 | solution.py:50
  665.1 11.7 cholesky.361
  678.1 9.8 custom-call.44
  690.2 11.7 cholesky.372
  703.3 9.8 custom-call.45
  714.9 11.9 cholesky.383
  728.1 9.8 custom-call.46
  742.5 134.9 %all-reduce.22.cloned.1.call-done = f32[128,128]{1,0:T(8,128)} async-done(((f32[128,128]{1,0:T(8,128)}), f32[128,128]{1,0:T(8,128)}) %all-reduce.22.cloned.1.call-update) | async-done | bytes 65552 | tf_op jit(solution)/shard_map/psum | solution.py:18
  878.0 65.6 %all-reduce.24.cloned.1.call-done = f32[128,128]{1,0:T(8,128)} async-done(((f32[128,128]{1,0:T(8,128)}), f32[128,128]{1,0:T(8,128)}) %all-reduce.24.cloned.1.call-update) | async-done | bytes 65552 | tf_op jit(solution)/shard_map/psum | solution.py:19
  946.0 4.6 collective-permute-start.8
  950.6 1.9 collective-permute-start.7
  953.0 2.2 fusion.36
  955.9 2.3 select_maximum_fusion
  958.2 4.4 fusion.39
  962.7 2.3 fusion.12
  965.0 263.4 %all-reduce.30.cloned.1.call-done = (f32[384,384]{1,0:T(8,128)}, f32[384,384]{0,1:T(8,128)}) async-done(((f32[384,384]{1,0:T(8,128)}, f32[384,384]{0,1:T(8,128)}), (f32[384,384]{1,0:T(8,128)}, f32[384,384]{0,1:T(8,128)})) %all-reduce.30.cloned.1.call-update) | async-done | bytes 1179664 | tf_op jit(solution)/shard_map/psum | solution.py:157
  1228.4 6.6 gather_fusion.1
  1237.7 11.7 cholesky.396
  1249.5 9.8 custom-call.48
  1261.7 11.7 cholesky.415
  1273.4 10.2 custom-call.49
  1285.0 11.7 cholesky.434
  1300.7 6.4 while.13
  1305.6 1.4 bitcast_dynamic-update-slice_fusion.5
  1307.0 29.7 %custom-call.55 = f32[3,128,128]{1,2,0:T(8,128)S(1)} custom-call(f32[3,128,128]{2,1,0:T(8,128)S(1)} %get-tuple-element.52), custom_call_target="InvertDiagBlocksLowerTriangular" | custom-call | tf_op jit(solution)/shard_map/triangular_solve/custom-call.8 | solution.py:50
  1344.2 11.7 cholesky.447
  1357.3 9.8 custom-call.52
  1369.1 11.7 cholesky.458
  1382.2 9.8 custom-call.53
  1393.8 11.9 cholesky.469
  1407.1 9.8 custom-call.54
  1418.9 1.4 broadcast_multiply_fusion
  1422.2 135.1 %all-reduce.26.cloned.1.call-done = f32[128,128]{1,0:T(8,128)} async-done(((f32[128,128]{1,0:T(8,128)}), f32[128,128]{1,0:T(8,128)}) %all-reduce.26.cloned.1.call-update) | async-done | bytes 65552 | tf_op jit(solution)/shard_map/psum | solution.py:18
  1557.3 9.0 all-to-all-start.2
  1566.2 57.4 %all-reduce.28.cloned.1.call-done = f32[128,128]{1,0:T(8,128)} async-done(((f32[128,128]{1,0:T(8,128)}), f32[128,128]{1,0:T(8,128)}) %all-reduce.28.cloned.1.call-update) | async-done | bytes 65552 | tf_op jit(solution)/shard_map/psum | solution.py:19
  (324 shorter events, 84.3 us)
Async XLA Ops:
  8.8 16.4 %all-to-all-start = ((f32[16,8,512]{2,0,1:T(8,128)}), f32[16,8,512]{2,0,1:T(8,128)S(1)}, u32[]{:S(2)}, u32[]{:S(2)}) async-start(f32[16,8,512]{2,0,1:T(8,128)} %bitcast.334), calls=%async_computation | async-start | bytes 524288 | tf_op jit(solution)/shard_map/all_to_all | solution.py:142
  16.2 8.8 collective-permute-start
  25.2 10.6 all-to-all-start.1
  29.3 166.4 %all-reduce.18.cloned.1.call-start = ((), (), s32[]{:S(2)}) async-start(), calls=%async_computation.3 | async-start | bytes 131072 | tf_op jit(solution)/shard_map/psum | solution.py:18
  29.5 12.1 collective-permute-start.2
  31.4 10.1 collective-permute-start.1
  35.1 13.9 copy-start.22
  35.1 13.9 copy-start.24
  35.1 13.9 copy-start.26
  35.1 13.9 copy-start.28
  35.2 13.9 copy-start.30
  35.2 13.9 copy-start.32
  35.2 13.9 copy-start.34
  35.8 160.0 %copy-start.36 = (f32[512]{0:T(512)}, f32[512]{0:T(512)S(1)}, u32[]{:S(2)}) copy-start(f32[512]{0:T(512)S(1)} %get-tuple-element.164) | copy-start | bytes 6148
  36.0 13.1 copy-start.15
  36.0 14.2 collective-permute-start.6
  38.9 11.3 collective-permute-start.5
  49.1 4.5 copy-start.16
  50.2 211.9 %all-reduce.20.cloned.1.call-start = ((), (), s32[]{:S(2)}) async-start(), calls=%async_computation.4 | async-start | bytes 131072 | tf_op jit(solution)/shard_map/psum | solution.py:19
  50.2 145.5 %copy-start.14 = (f32[128,1,2,256]{3,2,0,1:T(2,128)}, f32[128,1,2,256]{3,2,0,1:T(2,128)S(1)}, u32[]{:S(2)}) copy-start(f32[128,1,2,256]{3,2,0,1:T(2,128)S(1)} %collective-permute-done.6) | copy-start | bytes 786436
  195.7 354.9 %all-reduce.32.cloned.1.call-start = ((), (), s32[]{:S(2)}) async-start(), calls=%async_computation.10 | async-start | bytes 2359296 | tf_op jit(solution)/shard_map/psum | solution.py:157
  265.1 14.6 copy-start.17
  265.1 14.6 collective-permute-start.4
  269.9 9.9 collective-permute-start.3
  277.4 4.6 copy-start.23
  277.5 4.6 copy-start.25
  277.5 4.6 copy-start.27
  277.5 4.6 copy-start.29
  277.5 4.6 copy-start.31
  277.5 4.6 copy-start.33
  277.5 4.6 copy-start.35
  282.1 4.5 copy-start.37
  286.7 0.7 copy-start.6
  286.7 0.8 copy-start.8
  289.8 587.6 %all-reduce.22.cloned.1.call-start = ((), (), s32[]{:S(2)}) async-start(), calls=%async_computation.5 | async-start | bytes 131072 | tf_op jit(solution)/shard_map/psum | solution.py:18
  550.6 6.6 copy-start.2
  550.6 7.7 copy-start
  559.8 11.7 copy-start.12
  713.5 26.5 %copy-start.7 = (f32[128,512]{1,0:T(8,128)S(1)}, f32[128,512]{1,0:T(8,128)}, u32[]{:S(2)}) copy-start(f32[128,512]{1,0:T(8,128)} %copy-done.6) | copy-start | bytes 786436
  713.5 26.5 %copy-start.9 = (f32[128,512]{1,0:T(8,128)S(1)}, f32[128,512]{1,0:T(8,128)}, u32[]{:S(2)}) copy-start(f32[128,512]{1,0:T(8,128)} %copy-done.8) | copy-start | bytes 786436
  739.8 204.7 %copy-start.38 = (f32[512]{0:T(512)S(1)}, f32[512]{0:T(512)}, u32[]{:S(2)}) copy-start(f32[512]{0:T(512)} %get-tuple-element.163) | copy-start | bytes 6148
  740.7 222.0 %copy-start.4 = (f32[128,512]{1,0:T(8,128)}, f32[128,512]{1,0:T(8,128)S(1)}, u32[]{:S(2)}) copy-start(f32[128,512]{1,0:T(8,128)S(1)} %fusion.13) | copy-start | bytes 786436
  742.4 201.2 %all-reduce.24.cloned.1.call-start = ((), (), s32[]{:S(2)}) async-start(), calls=%async_computation.6 | async-start | bytes 131072 | tf_op jit(solution)/shard_map/psum | solution.py:19
  877.4 351.0 %all-reduce.30.cloned.1.call-start = ((), (), s32[]{:S(2)}) async-start(), calls=%async_computation.9 | async-start | bytes 2359296 | tf_op jit(solution)/shard_map/psum | solution.py:157
  878.0 84.7 %copy-start.10 = (f32[128,512]{1,0:T(8,128)}, f32[128,512]{1,0:T(8,128)S(1)}, u32[]{:S(2)}) copy-start(f32[128,512]{1,0:T(8,128)S(1)} %fusion.15) | copy-start | bytes 786436
  946.0 9.3 collective-permute-start.8
  950.6 5.2 collective-permute-start.7
  953.0 9.6 copy-start.18
  962.7 272.4 %copy-start.20 = (f32[128,512]{1,0:T(8,128)}, f32[128,512]{1,0:T(8,128)S(1)}, u32[]{:S(2)}) copy-start(f32[128,512]{1,0:T(8,128)S(1)} %multiply_subtract_fusion) | copy-start | bytes 786436
  965.0 592.3 %all-reduce.26.cloned.1.call-start = ((), (), s32[]{:S(2)}) async-start(), calls=%async_computation.7 | async-start | bytes 131072 | tf_op jit(solution)/shard_map/psum | solution.py:18
  1228.4 6.7 copy-start.3
  1228.4 7.7 copy-start.1
  1237.7 11.7 copy-start.13
  1392.0 26.9 %copy-start.11 = (f32[128,512]{1,0:T(8,128)S(1)}, f32[128,512]{1,0:T(8,128)}, u32[]{:S(2)}) copy-start(f32[128,512]{1,0:T(8,128)} %copy-done.10) | copy-start | bytes 786436
  1393.1 27.3 %copy-start.5 = (f32[128,512]{1,0:T(8,128)S(1)}, f32[128,512]{1,0:T(8,128)}, u32[]{:S(2)}) copy-start(f32[128,512]{1,0:T(8,128)} %copy-done.4) | copy-start | bytes 786436
  1393.1 27.2 %copy-start.19 = (f32[128,512]{1,0:T(8,128)S(1)}, f32[128,512]{1,0:T(8,128)}, u32[]{:S(2)}) copy-start(f32[128,512]{1,0:T(8,128)} %copy-done.18) | copy-start | bytes 786436
  1393.1 27.2 %copy-start.21 = (f32[128,512]{1,0:T(8,128)S(1)}, f32[128,512]{1,0:T(8,128)}, u32[]{:S(2)}) copy-start(f32[128,512]{1,0:T(8,128)} %copy-done.20) | copy-start | bytes 786436
  1422.1 201.5 %all-reduce.28.cloned.1.call-start = ((), (), s32[]{:S(2)}) async-start(), calls=%async_computation.8 | async-start | bytes 131072 | tf_op jit(solution)/shard_map/psum | solution.py:19
  1557.3 68.8 %all-to-all-start.2 = ((f32[8,16,512]{2,1,0:T(8,128)}), f32[8,16,512]{2,1,0:T(8,128)S(1)}, u32[]{:S(2)}, u32[]{:S(2)}) async-start(f32[8,16,512]{2,1,0:T(8,128)} %bitcast.87), calls=%async_computation.2 | async-start | bytes 524288 | tf_op jit(solution)/shard_map/all_to_all | solution.py:166
Sparse Core Ops, SparseCore 0:
  50.3 145.3 all-reduce.17
  198.0 63.9 all-reduce.19
  289.9 260.6 all-reduce.31
  742.6 134.8 all-reduce.21
  879.6 63.9 all-reduce.23
  965.1 263.2 all-reduce.29
  1422.2 134.9 all-reduce.25
  1559.6 63.9 all-reduce.27
